TPU v7x, 128 devices: a whole 4x4x4 slice. The times are simulated.
128 devices in a mesh: gx: 32 (over x, z, y_lo), gy: 4 (over y_hi, core).
Axes of the slice: x: 4, y: 4 (y_hi: 2, y_lo: 2; y = y_hi * 2 + y_lo), z: 4, core: 2. Of those that a mesh axis runs over, the one named last changes fastest.
Arguments:
- source_snaps: float32 [4, 1536, 64, 256], P(None, 'gx', 'gy'), may hold values from -6 to 6
- receiver_snaps: float32 [4, 1536, 64, 256], P(None, 'gx', 'gy'), may hold values from -6 to 6
- snap_pairs: int32 [3, 2], replicated, may hold values from 0 to 3
- offset_lags: int32 [17], replicated, may hold values from -24 to 24, as said below
- weight_table: float32 [4, 17], replicated, may hold values from 0.2 to 1
- weight_index: int32 [3], replicated, may hold values from 0 to 3
Outputs:
- adjoint_source: float32 [3, 1536, 64, 256], P(None, 'gx', 'gy')
- adjoint_receiver: float32 [3, 1536, 64, 256], P(None, 'gx', 'gy')
Inputs may be any that keep to these rules, and one draw needn't show every extreme that they name: `offset_lags`: strictly increasing; the first entry is -24 and the last is 24.
All inputs are finite; a program needn't handle non-finite values.
Results may differ from a plain program's by a relative error of at most 0.00002.
Values sent between devices are 32-bit elements; how exact they have to be, the bound alone decides.
No kernel may reach another device: no remote copies, remote signals or barrier semaphores. Data moves between devices by JAX's collectives and lax.ppermute only.
A program may use at most 128 MiB of HBM per device.

v0:
```python
import jax
import jax.numpy as jnp
from jax import lax
from jax.sharding import PartitionSpec as P

NOFF = 17
MAXLAG = 24


def with_halo(block, sides, width):
    for axis, dim in sides:
        count = lax.axis_size(axis)
        forward = [(i, i + 1) for i in range(count - 1)]
        backward = [(target, source) for source, target in forward]
        low = lax.ppermute(
            lax.slice_in_dim(block, block.shape[dim] - width, None, axis=dim), axis, forward
        )
        high = lax.ppermute(lax.slice_in_dim(block, 0, width, axis=dim), axis, backward)
        block = jnp.concatenate([low, block, high], axis=dim)
    return block


def passed_along(block, axis, distance):
    devices = range(lax.axis_size(axis))
    route = [(i - distance, i) for i in devices if i - distance in devices]
    return lax.ppermute(block, axis, route)


def smooth_pairs(values):
    return (
        values[:, :, :-4]
        + values[:, :, 4:]
        + 4.0 * (values[:, :, 1:-3] + values[:, :, 3:-1])
        + 6.0 * values[:, :, 2:-2]
    ) / 16.0


def place_add(totals, values, start):
    current = lax.dynamic_slice_in_dim(totals, start, values.shape[1], 1)
    return lax.dynamic_update_slice_in_dim(totals, current + values, start, 1)


def local(source_snaps, receiver_snaps, snap_pairs, offset_lags, weight_table, weight_index):
    cells_x = source_snaps.shape[1]
    cells_y = source_snaps.shape[2]
    depth = source_snaps.shape[3]
    pair_count = snap_pairs.shape[0]
    chosen = [source_snaps[snap_pairs[pair_index, 0]] for pair_index in range(pair_count)]
    chosen = chosen + [
        receiver_snaps[snap_pairs[pair_index, 1]] for pair_index in range(pair_count)
    ]
    fields = jnp.stack(chosen)
    widened = with_halo(fields, (("gy", 2),), 2)
    pair_weights = weight_table[weight_index]
    extended = with_halo(widened, (("gx", 1),), MAXLAG)
    source_wide = extended[:pair_count]
    receiver_wide = extended[pair_count:]

    def step(offset, running):
        source_total, receiver_total = running
        offset_lag = offset_lags[offset]
        weight = pair_weights[:, offset][:, None, None, None]
        shifted_source = lax.dynamic_slice_in_dim(source_wide, MAXLAG - offset_lag, cells_x, 1)
        shifted_receiver = lax.dynamic_slice_in_dim(receiver_wide, MAXLAG + offset_lag, cells_x, 1)
        smoothed = smooth_pairs(weight * shifted_source * shifted_receiver)
        source_total = place_add(
            source_total, smoothed * shifted_receiver[:, :, 2:-2], MAXLAG - offset_lag
        )
        receiver_total = place_add(
            receiver_total, smoothed * shifted_source[:, :, 2:-2], MAXLAG + offset_lag
        )
        return (source_total, receiver_total)

    zeros = jnp.zeros((pair_count, cells_x + 2 * MAXLAG, cells_y, depth), jnp.float32)
    source_total, receiver_total = lax.fori_loop(0, NOFF, step, (zeros, zeros))
    totals = jnp.concatenate([source_total, receiver_total], axis=0)
    from_above = passed_along(totals[:, :MAXLAG], "gx", -1)
    from_below = passed_along(totals[:, cells_x + MAXLAG :], "gx", 1)
    owned = totals[:, MAXLAG : cells_x + MAXLAG]
    owned = owned.at[:, :MAXLAG].add(from_below)
    owned = owned.at[:, cells_x - MAXLAG :].add(from_above)
    return (owned[:pair_count], owned[pair_count:])


def solution(mesh):
    return jax.shard_map(
        local,
        mesh=mesh,
        in_specs=(P(None, "gx", "gy", None), P(None, "gx", "gy", None), P(), P(), P(), P()),
        out_specs=(P(None, "gx", "gy", None), P(None, "gx", "gy", None)),
        check_vma=False,
    )
```

profile of v0, /device:TPU:7, one launch (start us, length us, event | category | flops | bytes accessed | tf_op | source)
XLA Modules:
  0.0 590.0 jit_solution(7171743871562934684)
XLA Ops:
  23.5 5.4 collective-permute-start
  30.8 4.9 collective-permute-done
  35.6 6.9 %collective-permute-done.1 = f32[6,48,2,256]{3,1,2,0:T(8,128)S(1)} collective-permute-done((f32[6,48,2,256]{3,1,2,0:T(8,128)S(1)}, f32[6,48,2,256]{3,1,2,0:T(8,128)S(1)}, u32[]{:S(2)}, u32[]{:S(2)}) %collective-permute-start.1) | collective-permute-done | bytes 589856 | tf_op jit(solution)/shard_map/ppermute | solution.py:18
  43.3 3.2 fusion.15
  48.4 39.1 %collective-permute-start.3 = (f32[6,24,20,256]{3,1,2,0:T(8,128)}, f32[6,24,20,256]{3,1,2,0:T(8,128)}, u32[]{:S(2)}, u32[]{:S(2)}) collective-permute-start(f32[6,24,20,256]{3,1,2,0:T(8,128)} %get-tuple-element.265), channel_id=1, source_target_pairs={{4,0},{8,4},{12,8},{16,12},{20,16},{24,20},{28,24},{32,28},{36,32}... | collective-permute-start | bytes 8847368 | tf_op jit(solution)/shard_map/ppermute | solution.py:18
  89.5 28.8 %collective-permute-done.2 = f32[6,24,20,256]{3,1,2,0:T(8,128)S(1)} collective-permute-done((f32[6,24,20,256]{3,1,2,0:T(8,128)}, f32[6,24,20,256]{3,1,2,0:T(8,128)S(1)}, u32[]{:S(2)}, u32[]{:S(2)}) %collective-permute-start.2) | collective-permute-done | bytes 2949152 | tf_op jit(solution)/shard_map/ppermute | solution.py:15
  118.3 51.3 %collective-permute-done.3 = f32[6,24,20,256]{3,1,2,0:T(8,128)} collective-permute-done((f32[6,24,20,256]{3,1,2,0:T(8,128)}, f32[6,24,20,256]{3,1,2,0:T(8,128)}, u32[]{:S(2)}, u32[]{:S(2)}) %collective-permute-start.3) | collective-permute-done | bytes 2949152 | tf_op jit(solution)/shard_map/ppermute | solution.py:18
  169.6 8.6 %pad_maximum_fusion = f32[6,96,20,256]{3,1,2,0:T(8,128)} fusion(f32[6,24,20,256]{3,1,2,0:T(8,128)} %collective-permute-done.3, f32[6,48,2,256]{3,1,2,0:T(8,128)} %copy-done.7, f32[6,48,16,256]{3,1,2,0:T(8,128)} %copy-done.6, f32[6,48,2,256]{3,1,2,0:T(8,128)S(1)} %collective-permute-done, f32[6,24,20,256]{3,1,2,0:T(8,128)S(1)} %collective-permute-done.2), kind=kLoop, calls=%fused_computation.19 | loop fusion | flops 11796480 | bytes 23592960 | tf_op jit(solution)/shard_map/concatenate | solution.py:19
  178.1 10.2 %fusion.13 = (f32[3,96,20,256]{3,1,2,0:T(8,128)}, f32[3,96,20,256]{3,1,2,0:T(8,128)}) fusion(f32[6,96,20,256]{3,1,2,0:T(8,128)} %pad_maximum_fusion), kind=kLoop, calls=%fused_computation.42 | loop fusion | bytes 23592960 | tf_op jit(solution)/shard_map/slice | solution.py:57
  188.3 2.8 broadcast_in_dim.6.clone
  191.1 2.7 broadcast_in_dim.6
  193.9 288.6 %while.20 = (s32[]{:T(128)}, f32[3,96,16,256]{3,2,1,0:T(8,128)}, f32[3,96,16,256]{3,2,1,0:T(8,128)}, s32[17]{0:T(128)S(1)}, f32[3,17]{0,1:T(8,128)S(1)}, /*index...) while((s32[]{:T(128)}, f32[3,96,16,256]{3,2,1,0:T(8,128)}, ...), condition=%wide.region_1.0_spmd, body=%wide.region_0.0_spmd.sunk | while | flops 7962634 | bytes 123273640 | solution.py:75
  197.1 4.0 constant_dynamic-slice_fusion.10
  201.1 3.6 fusion.24
  208.6 2.1 copy-done.4
  213.9 4.1 constant_dynamic-slice_fusion.10
  218.1 3.6 fusion.24
  225.6 2.1 copy-done.4
  230.9 4.1 constant_dynamic-slice_fusion.10
  235.1 3.6 fusion.24
  242.6 2.1 copy-done.4
  247.9 4.1 constant_dynamic-slice_fusion.10
  252.1 3.6 fusion.24
  259.6 2.1 copy-done.4
  264.9 4.1 constant_dynamic-slice_fusion.10
  269.1 3.6 fusion.24
  276.6 2.1 copy-done.4
  281.9 4.1 constant_dynamic-slice_fusion.10
  286.1 3.6 fusion.24
  293.6 2.1 copy-done.4
  298.9 4.1 constant_dynamic-slice_fusion.10
  303.1 3.6 fusion.24
  310.6 2.1 copy-done.4
  315.9 4.1 constant_dynamic-slice_fusion.10
  320.1 3.6 fusion.24
  327.6 2.1 copy-done.4
  332.9 4.1 constant_dynamic-slice_fusion.10
  337.1 3.6 fusion.24
  344.5 2.1 copy-done.4
  349.9 4.1 constant_dynamic-slice_fusion.10
  354.1 3.6 fusion.24
  361.5 2.1 copy-done.4
  366.9 4.1 constant_dynamic-slice_fusion.10
  371.1 3.6 fusion.24
  378.5 2.1 copy-done.4
  383.9 4.1 constant_dynamic-slice_fusion.10
  388.1 3.6 fusion.24
  395.5 2.1 copy-done.4
  400.9 4.1 constant_dynamic-slice_fusion.10
  405.0 3.6 fusion.24
  417.9 4.1 constant_dynamic-slice_fusion.10
  422.0 3.6 fusion.24
  434.9 4.1 constant_dynamic-slice_fusion.10
  439.0 3.6 fusion.24
  451.9 4.1 constant_dynamic-slice_fusion.10
  456.0 3.6 fusion.24
  468.9 4.0 constant_dynamic-slice_fusion.10
  472.9 3.6 fusion.24
  482.5 3.0 constant_dynamic-update-slice_fusion.1
  487.6 2.3 collective-permute-start.4
  489.9 6.0 %collective-permute-start.5 = (f32[6,24,16,256]{3,2,1,0:T(8,128)S(1)}, f32[6,24,16,256]{3,2,1,0:T(8,128)S(1)}, u32[]{:S(2)}, u32[]{:S(2)}) collective-permute-start(f32[6,24,16,256]{3,2,1,0:T(8,128)S(1)} %get-tuple-element.262), channel_id=1, source_target_pairs={{4,0},{8,4},{12,8},{16,12},{20,16},{24,20},{28,24},{32,28},{36,32}... | collective-permute-start | bytes 7077896 | tf_op jit(solution)/shard_map/ppermute | solution.py:26
  496.9 40.5 %collective-permute-done.4 = f32[6,24,16,256]{3,2,1,0:T(8,128)S(1)} collective-permute-done((f32[6,24,16,256]{3,2,1,0:T(8,128)S(1)}, f32[6,24,16,256]{3,2,1,0:T(8,128)S(1)}, u32[]{:S(2)}, u32[]{:S(2)}) %collective-permute-start.4) | collective-permute-done | bytes 2359328 | tf_op jit(solution)/shard_map/ppermute | solution.py:26
  537.9 48.2 %collective-permute-done.5 = f32[6,24,16,256]{3,2,1,0:T(8,128)S(1)} collective-permute-done((f32[6,24,16,256]{3,2,1,0:T(8,128)S(1)}, f32[6,24,16,256]{3,2,1,0:T(8,128)S(1)}, u32[]{:S(2)}, u32[]{:S(2)}) %collective-permute-start.5) | collective-permute-done | bytes 2359328 | tf_op jit(solution)/shard_map/ppermute | solution.py:26
  586.8 3.2 fusion.16
  (334 shorter events, 107.3 us)
Async XLA Ops:
  0.6 87.0 %copy-start = (f32[4,17]{1,0:T(4,128)S(1)}, f32[4,17]{1,0:T(4,128)}, u32[]{:S(2)}) copy-start(f32[4,17]{1,0:T(4,128)} %param.16) | copy-start | bytes 820
  16.9 2.7 copy-start.8
  23.3 19.9 %copy-start.6 = (f32[6,48,16,256]{3,1,2,0:T(8,128)}, f32[6,48,16,256]{3,1,2,0:T(8,128)S(1)}, u32[]{:S(2)}) copy-start(f32[6,48,16,256]{3,1,2,0:T(8,128)S(1)} %copy_dynamic-update-slice_fusion) | copy-start | bytes 14155780
  23.5 12.2 %collective-permute-start = (f32[6,48,2,256]{3,1,2,0:T(8,128)S(1)}, f32[6,48,2,256]{3,1,2,0:T(8,128)S(1)}, u32[]{:S(2)}, u32[]{:S(2)}) collective-permute-start(f32[6,48,2,256]{3,1,2,0:T(8,128)S(1)} %get-tuple-element.268), channel_id=1, source_target_pairs={{0,1},{1,2},{2,3},{4,5},{5,6},{6,7},{8,9},{9,10},{10,11},{12,13},{... | collective-permute-start | bytes 1769480 | tf_op jit(solution)/shard_map/ppermute | solution.py:15
  28.8 13.7 %collective-permute-start.1 = (f32[6,48,2,256]{3,1,2,0:T(8,128)S(1)}, f32[6,48,2,256]{3,1,2,0:T(8,128)S(1)}, u32[]{:S(2)}, u32[]{:S(2)}) collective-permute-start(f32[6,48,2,256]{3,1,2,0:T(8,128)S(1)} %get-tuple-element.269), channel_id=1, source_target_pairs={{1,0},{2,1},{3,2},{5,4},{6,5},{7,6},{9,8},{10,9},{11,10},{13,12},{... | collective-permute-start | bytes 1769480 | tf_op jit(solution)/shard_map/ppermute | solution.py:18
  43.3 44.2 %copy-start.9 = (s32[3]{0:T(128)S(1)}, s32[3]{0:T(128)}, u32[]{:S(2)}) copy-start(s32[3]{0:T(128)} %param.17) | copy-start | bytes 40
  46.5 71.8 %collective-permute-start.2 = (f32[6,24,20,256]{3,1,2,0:T(8,128)}, f32[6,24,20,256]{3,1,2,0:T(8,128)S(1)}, u32[]{:S(2)}, u32[]{:S(2)}) collective-permute-start(f32[6,24,20,256]{3,1,2,0:T(8,128)} %get-tuple-element.264), channel_id=1, source_target_pairs={{0,4},{4,8},{8,12},{12,16},{16,20},{20,24},{24,28},{28,32},{32,36}... | collective-permute-start | bytes 8847368 | tf_op jit(solution)/shard_map/ppermute | solution.py:15
  48.4 121.2 %collective-permute-start.3 = (f32[6,24,20,256]{3,1,2,0:T(8,128)}, f32[6,24,20,256]{3,1,2,0:T(8,128)}, u32[]{:S(2)}, u32[]{:S(2)}) collective-permute-start(f32[6,24,20,256]{3,1,2,0:T(8,128)} %get-tuple-element.265), channel_id=1, source_target_pairs={{4,0},{8,4},{12,8},{16,12},{20,16},{24,20},{28,24},{32,28},{36,32}... | collective-permute-start | bytes 8847368 | tf_op jit(solution)/shard_map/ppermute | solution.py:18
  188.3 5.5 copy-start.10
  197.1 7.7 %slice-start = ((s8[4718592]{0:T(1024)(128)(4,1)}), s8[4194304]{0:T(1024)(128)(4,1)S(1)}, s32[]{:S(2)}) async-start(s8[4718592]{0:T(1024)(128)(4,1)} %bitcast.22), calls=%async_computation | async-start | bytes 8388608 | tf_op jit(solution)/shard_map/while
  201.1 3.7 slice-start.1
  201.1 5.3 slice-start.2
  213.9 7.8 %slice-start = ((s8[4718592]{0:T(1024)(128)(4,1)}), s8[4194304]{0:T(1024)(128)(4,1)S(1)}, s32[]{:S(2)}) async-start(s8[4718592]{0:T(1024)(128)(4,1)} %bitcast.22), calls=%async_computation | async-start | bytes 8388608 | tf_op jit(solution)/shard_map/while
  218.1 3.7 slice-start.1
  218.1 5.3 slice-start.2
  230.9 7.8 %slice-start = ((s8[4718592]{0:T(1024)(128)(4,1)}), s8[4194304]{0:T(1024)(128)(4,1)S(1)}, s32[]{:S(2)}) async-start(s8[4718592]{0:T(1024)(128)(4,1)} %bitcast.22), calls=%async_computation | async-start | bytes 8388608 | tf_op jit(solution)/shard_map/while
  235.1 3.7 slice-start.1
  235.1 5.3 slice-start.2
  247.9 7.8 %slice-start = ((s8[4718592]{0:T(1024)(128)(4,1)}), s8[4194304]{0:T(1024)(128)(4,1)S(1)}, s32[]{:S(2)}) async-start(s8[4718592]{0:T(1024)(128)(4,1)} %bitcast.22), calls=%async_computation | async-start | bytes 8388608 | tf_op jit(solution)/shard_map/while
  252.1 3.7 slice-start.1
  252.1 5.3 slice-start.2
  264.9 7.8 %slice-start = ((s8[4718592]{0:T(1024)(128)(4,1)}), s8[4194304]{0:T(1024)(128)(4,1)S(1)}, s32[]{:S(2)}) async-start(s8[4718592]{0:T(1024)(128)(4,1)} %bitcast.22), calls=%async_computation | async-start | bytes 8388608 | tf_op jit(solution)/shard_map/while
  269.1 3.7 slice-start.1
  269.1 5.3 slice-start.2
  281.9 7.8 %slice-start = ((s8[4718592]{0:T(1024)(128)(4,1)}), s8[4194304]{0:T(1024)(128)(4,1)S(1)}, s32[]{:S(2)}) async-start(s8[4718592]{0:T(1024)(128)(4,1)} %bitcast.22), calls=%async_computation | async-start | bytes 8388608 | tf_op jit(solution)/shard_map/while
  286.1 3.7 slice-start.1
  286.1 5.3 slice-start.2
  298.9 7.8 %slice-start = ((s8[4718592]{0:T(1024)(128)(4,1)}), s8[4194304]{0:T(1024)(128)(4,1)S(1)}, s32[]{:S(2)}) async-start(s8[4718592]{0:T(1024)(128)(4,1)} %bitcast.22), calls=%async_computation | async-start | bytes 8388608 | tf_op jit(solution)/shard_map/while
  303.1 3.7 slice-start.1
  303.1 5.3 slice-start.2
  315.9 7.8 %slice-start = ((s8[4718592]{0:T(1024)(128)(4,1)}), s8[4194304]{0:T(1024)(128)(4,1)S(1)}, s32[]{:S(2)}) async-start(s8[4718592]{0:T(1024)(128)(4,1)} %bitcast.22), calls=%async_computation | async-start | bytes 8388608 | tf_op jit(solution)/shard_map/while
  320.1 3.7 slice-start.1
  320.1 5.3 slice-start.2
  332.9 7.8 %slice-start = ((s8[4718592]{0:T(1024)(128)(4,1)}), s8[4194304]{0:T(1024)(128)(4,1)S(1)}, s32[]{:S(2)}) async-start(s8[4718592]{0:T(1024)(128)(4,1)} %bitcast.22), calls=%async_computation | async-start | bytes 8388608 | tf_op jit(solution)/shard_map/while
  337.0 3.7 slice-start.1
  337.1 5.3 slice-start.2
  349.9 7.8 %slice-start = ((s8[4718592]{0:T(1024)(128)(4,1)}), s8[4194304]{0:T(1024)(128)(4,1)S(1)}, s32[]{:S(2)}) async-start(s8[4718592]{0:T(1024)(128)(4,1)} %bitcast.22), calls=%async_computation | async-start | bytes 8388608 | tf_op jit(solution)/shard_map/while
  354.0 3.7 slice-start.1
  354.1 5.3 slice-start.2
  366.9 7.8 %slice-start = ((s8[4718592]{0:T(1024)(128)(4,1)}), s8[4194304]{0:T(1024)(128)(4,1)S(1)}, s32[]{:S(2)}) async-start(s8[4718592]{0:T(1024)(128)(4,1)} %bitcast.22), calls=%async_computation | async-start | bytes 8388608 | tf_op jit(solution)/shard_map/while
  371.0 3.7 slice-start.1
  371.0 5.3 slice-start.2
  383.9 7.8 %slice-start = ((s8[4718592]{0:T(1024)(128)(4,1)}), s8[4194304]{0:T(1024)(128)(4,1)S(1)}, s32[]{:S(2)}) async-start(s8[4718592]{0:T(1024)(128)(4,1)} %bitcast.22), calls=%async_computation | async-start | bytes 8388608 | tf_op jit(solution)/shard_map/while
  388.0 3.7 slice-start.1
  388.0 5.3 slice-start.2
  400.9 7.8 %slice-start = ((s8[4718592]{0:T(1024)(128)(4,1)}), s8[4194304]{0:T(1024)(128)(4,1)S(1)}, s32[]{:S(2)}) async-start(s8[4718592]{0:T(1024)(128)(4,1)} %bitcast.22), calls=%async_computation | async-start | bytes 8388608 | tf_op jit(solution)/shard_map/while
  405.0 3.7 slice-start.1
  405.0 5.3 slice-start.2
  417.9 7.8 %slice-start = ((s8[4718592]{0:T(1024)(128)(4,1)}), s8[4194304]{0:T(1024)(128)(4,1)S(1)}, s32[]{:S(2)}) async-start(s8[4718592]{0:T(1024)(128)(4,1)} %bitcast.22), calls=%async_computation | async-start | bytes 8388608 | tf_op jit(solution)/shard_map/while
  422.0 3.7 slice-start.1
  422.0 5.3 slice-start.2
  434.9 7.8 %slice-start = ((s8[4718592]{0:T(1024)(128)(4,1)}), s8[4194304]{0:T(1024)(128)(4,1)S(1)}, s32[]{:S(2)}) async-start(s8[4718592]{0:T(1024)(128)(4,1)} %bitcast.22), calls=%async_computation | async-start | bytes 8388608 | tf_op jit(solution)/shard_map/while
  439.0 3.7 slice-start.1
  439.0 5.3 slice-start.2
  451.9 7.8 %slice-start = ((s8[4718592]{0:T(1024)(128)(4,1)}), s8[4194304]{0:T(1024)(128)(4,1)S(1)}, s32[]{:S(2)}) async-start(s8[4718592]{0:T(1024)(128)(4,1)} %bitcast.22), calls=%async_computation | async-start | bytes 8388608 | tf_op jit(solution)/shard_map/while
  456.0 3.7 slice-start.1
  456.0 5.3 slice-start.2
  468.8 7.7 %slice-start = ((s8[4718592]{0:T(1024)(128)(4,1)}), s8[4194304]{0:T(1024)(128)(4,1)S(1)}, s32[]{:S(2)}) async-start(s8[4718592]{0:T(1024)(128)(4,1)} %bitcast.22), calls=%async_computation | async-start | bytes 8388608 | tf_op jit(solution)/shard_map/while
  472.9 3.7 slice-start.1
  472.9 5.3 slice-start.2
  482.5 3.8 copy-start.3
  487.6 49.8 %collective-permute-start.4 = (f32[6,24,16,256]{3,2,1,0:T(8,128)S(1)}, f32[6,24,16,256]{3,2,1,0:T(8,128)S(1)}, u32[]{:S(2)}, u32[]{:S(2)}) collective-permute-start(f32[6,24,16,256]{3,2,1,0:T(8,128)S(1)} %get-tuple-element.263), channel_id=1, source_target_pairs={{0,4},{4,8},{8,12},{12,16},{16,20},{20,24},{24,28},{28,32},{32,36}... | collective-permute-start | bytes 7077896 | tf_op jit(solution)/shard_map/ppermute | solution.py:26
  489.9 96.3 %collective-permute-start.5 = (f32[6,24,16,256]{3,2,1,0:T(8,128)S(1)}, f32[6,24,16,256]{3,2,1,0:T(8,128)S(1)}, u32[]{:S(2)}, u32[]{:S(2)}) collective-permute-start(f32[6,24,16,256]{3,2,1,0:T(8,128)S(1)} %get-tuple-element.262), channel_id=1, source_target_pairs={{4,0},{8,4},{12,8},{16,12},{20,16},{24,20},{28,24},{32,28},{36,32}... | collective-permute-start | bytes 7077896 | tf_op jit(solution)/shard_map/ppermute | solution.py:26
  586.2 3.8 copy-start.1
  (53 other events, 114.0 us)
where the time goes:
time: 593 us; the launch traced here: 590 us
  waiting for transfers between devices  181 us (31%)
  local copies, waits for them, and re-layouts  175 us (30%)
  other arithmetic  119 us (20%)
  starting transfers between devices  56.6 us (10%)
  loops' own time  46 us (8%)
  between operations  12.3 us (2%)
    ppermute x2, waiting for transfers between devices, passed_along(): return lax.ppermute(block, axis, route)  88.7 us
    dynamic_slice x17, local copies, waits for them, and re-layouts, step(): lax.dynamic_slice_in_dim(receiver_wide, MAXLAG + offset_lag, cells_x, 1)  70.1 us
    dynamic_slice x17, other arithmetic, step(): lax.dynamic_slice_in_dim(receiver_wide, MAXLAG + offset_lag, cells_x, 1)  61.6 us
    ppermute x2, waiting for transfers between devices, with_halo(): lax.ppermute(lax.slice_in_dim(block, 0, width, axis=dim), axis, backward)  58.1 us
    while x204, local copies, waits for them, and re-layouts  53.9 us
    dynamic_update_slice x34, other arithmetic, place_add(): return lax.dynamic_update_slice_in_dim(totals, current + values, start, 1)  46.9 us
    another operation x1, loops' own time, local(): source_total, receiver_total = lax.fori_loop(0, NOFF, step, (zeros, zeros))  46 us
    ppermute x2, starting transfers between devices, with_halo(): lax.ppermute(lax.slice_in_dim(block, 0, width, axis=dim), axis, backward)  41.1 us
  transfers between devices with their start and end apart: 6, of which 6 were waited for; matrix products, arithmetic and copies ran while one was open for 1% of the time, Pallas kernels for 0%

commit v1 on v0

v1 whole, which is shorter than its diff:
```python
import functools

import jax
import jax.numpy as jnp
from jax import lax
from jax.experimental import pallas as pl
from jax.experimental.pallas import tpu as pltpu
from jax.sharding import PartitionSpec as P

F32 = jnp.float32


def moves(mesh):
    nx, ny = mesh.shape["gx"], mesh.shape["gy"]
    flat = lambda x, y: x * ny + y
    middle = [y for y in range(ny) if y not in (0, ny - 1)]
    across = [(x, x ^ 1) for x in range(nx) if x ^ 1 < nx]
    onward = [(x, x + 2) for x in range(0, nx - 2, 2)] + [(x, x - 2) for x in range(3, nx, 2)]
    whole = lambda route, rows: [(flat(a, y), flat(b, y)) for a, b in route for y in rows]
    twins = [(flat(x, y), flat(x, y ^ 1)) for x in range(nx) for y in range(ny)]
    seam = [(flat(x, a), flat(x, b)) for x in range(nx) for y in range(1, ny - 1, 2) for a, b in ((y, y + 1), (y + 1, y))]
    return {
        "across": whole(across, range(ny)),
        "onward": whole(onward, range(ny)),
        "across_edge": whole(across, middle),
        "onward_edge": whole(onward, middle),
        "twins": twins,
        "seam": seam,
    }


def image_kernel(
    place, lags, weights, user, own, near, far, own_twin, own_edge, near_twin, near_edge, far_twin, far_edge,
    mate, mate_twin, mate_edge, out, ext, prod, mix, mext, done, sems,
):
    cells, rows, _ = own.shape
    odd, second = place[0], place[1]
    near_at = jnp.where(odd == 1, 0, 2 * cells)
    far_at = jnp.where(odd == 1, 2 * cells, 0)
    spots = ((own, cells, own_twin, own_edge), (near, near_at, near_twin, near_edge), (far, far_at, far_twin, far_edge))

    def fill(index, block, target, at):
        return pltpu.make_async_copy(block, target.at[pl.ds(at, cells), pl.ds(8, rows)], sems.at[index])

    copies = [fill(i, spot[0], ext, spot[1]) for i, spot in enumerate(spots)] + [fill(3, mate, mext, 0)]
    for copy in copies:
        copy.start()
    low_tile = lax.broadcasted_iota(jnp.int32, (8, ext.shape[2]), 0)

    def edges(x, twin, edge):
        t, e = twin[x], edge[x]
        return jnp.where(second == 1, t, e), jnp.where(second == 1, e, t)

    for i, (_, at, twin, edge) in enumerate(spots):
        copies[i].wait()

        def product(x, carry):
            low, high = edges(x, twin, edge)
            ext[at + x, 6:8] = low
            ext[at + x, rows + 8 : rows + 10] = high
            here = ext[at + x, 8 : rows + 8]
            prod[at + x, 0:rows] = here * here
            prod[at + x, rows : 2 * rows] = here * ext[at + x, 9 : rows + 9]
            prod[at + x, 2 * rows : 3 * rows] = here * ext[at + x, 10 : rows + 10]
            base = ext[at + x, 0:8]
            one = base * ext[at + x, 1:9]
            two = base * ext[at + x, 2:10]
            prod[at + x, 3 * rows : 3 * rows + 8] = jnp.where(low_tile >= 6, two, pltpu.roll(one, 6, 0))
            return carry

        lax.fori_loop(0, cells, product, 0, unroll=2)

    copies[3].wait()
    count = lags.shape[0]

    def total(x, carry):
        low, high = edges(x, mate_twin, mate_edge)
        mext[x, 6:8] = low
        mext[x, rows + 8 : rows + 10] = high
        acc = None
        for h in range(count):
            term = weights[h] * prod[x + lags[h]]
            acc = term if acc is None else acc + term
        mix[0, 8 : rows + 8] = acc[rows : 2 * rows]
        mix[1, 8 : rows + 8] = acc[2 * rows : 3 * rows]
        extra = acc[3 * rows : 3 * rows + 8]
        mix[0, 0:8] = pltpu.roll(extra, 2, 0)
        mix[1, 0:8] = extra
        done[x] = (
            0.375 * (acc[0:rows] * mext[x, 8 : rows + 8])
            + 0.25 * (acc[rows : 2 * rows] * mext[x, 9 : rows + 9] + mix[0, 7 : rows + 7] * mext[x, 7 : rows + 7])
            + 0.0625 * (acc[2 * rows : 3 * rows] * mext[x, 10 : rows + 10] + mix[1, 6 : rows + 6] * mext[x, 6 : rows + 6])
        )
        return carry

    lax.fori_loop(0, cells, total, 0)
    out[...] = done[...]


def image(place, lags, weights, own, near, far, halos, mate, mate_halos):
    cells, rows, depth = own.shape
    smem = pl.BlockSpec(memory_space=pltpu.SMEM)
    vmem = pl.BlockSpec(memory_space=pltpu.VMEM)
    hbm = pl.BlockSpec(memory_space=pl.ANY)
    user = jnp.zeros((1,), jnp.int32)
    return pl.pallas_call(
        image_kernel,
        out_shape=jax.ShapeDtypeStruct((cells, rows, depth), F32),
        in_specs=[smem] * 4 + [hbm] * 3 + [vmem] * 6 + [hbm] + [vmem] * 2,
        out_specs=vmem,
        scratch_shapes=[
            pltpu.VMEM((3 * cells, rows + 16, depth), F32),
            pltpu.VMEM((3 * cells, 3 * rows + 8, depth), F32),
            pltpu.VMEM((2, rows + 8, depth), F32),
            pltpu.VMEM((cells, rows + 16, depth), F32),
            pltpu.VMEM((cells, rows, depth), F32),
            pltpu.SemaphoreType.DMA((4,)),
        ],
        compiler_params=pltpu.CompilerParams(vmem_limit_bytes=40 * 2**20),
        cost_estimate=pl.CostEstimate(flops=22 * 10**6, bytes_accessed=4 * 10**6, transcendentals=0),
    )(place, lags, weights, user, own, near, far, *halos, mate, *mate_halos)


def local(routes, source_snaps, receiver_snaps, snap_pairs, offset_lags, weight_table, weight_index):
    pairs = snap_pairs.shape[0]
    cells = source_snaps.shape[1]
    rows = source_snaps.shape[2]
    send = lambda value, route: lax.ppermute(value, ("gx", "gy"), routes[route])
    odd = lax.axis_index("gx") % 2
    second = lax.axis_index("gy") % 2
    place = jnp.stack([odd, second]).astype(jnp.int32)

    fields = []
    for p in range(pairs):
        fields.append(receiver_snaps[snap_pairs[p, 1]])
        fields.append(source_snaps[snap_pairs[p, 0]])
    n = len(fields)

    def toward(block, near_twin):
        low, high = block[:, :2], block[:, rows - 2 :]
        return jnp.where((second == 0) == near_twin, high, low)

    own_twin = send(jnp.stack([toward(f, True) for f in fields]), "twins")
    own_edge = send(jnp.stack([toward(f, False) for f in fields]), "seam")
    near_edge = send(own_edge, "across_edge")
    far_edge = send(near_edge, "onward_edge")

    near, far, near_twin, far_twin = [], [], [], []
    for f in fields:
        near.append(send(f, "across"))
        far.append(send(near[-1], "onward"))
        near_twin.append(send(toward(near[-1], True), "twins"))
        far_twin.append(send(toward(far[-1], True), "twins"))

    outs = []
    for u in range(n):
        p, mate = u // 2, u ^ 1
        sign = 2 if u % 2 == 0 else -2
        outs.append(
            image(
                place,
                cells + sign * offset_lags,
                weight_table[weight_index[p]],
                fields[u],
                near[u],
                far[u],
                (own_twin[u], own_edge[u], near_twin[u], near_edge[u], far_twin[u], far_edge[u]),
                fields[mate],
                (own_twin[mate], own_edge[mate]),
            )
        )
    return jnp.stack(outs[0::2]), jnp.stack(outs[1::2])


def solution(mesh):
    routes = moves(mesh)
    split = P(None, "gx", "gy", None)
    return jax.shard_map(
        functools.partial(local, routes),
        mesh=mesh,
        in_specs=(split, split, P(), P(), P(), P()),
        out_specs=(split, split),
        check_vma=False,
    )
```

time: 593 us -> 264 us (0.45)
  local copies, waits for them, and re-layouts: 175 us -> 9.83 us
  other arithmetic: 119 us -> 13.1 us
  loops' own time: 46 us -> 0 us
  Pallas kernels: 0 us -> 42.1 us
  waiting for transfers between devices: 181 us -> 143 us
  starting transfers between devices: 56.6 us -> 37.9 us
    dynamic_slice x36 -> x0, local copies, waits for them, and re-layouts: 82 us -> none  [the longest x17 70.1 us: step(): lax.dynamic_slice_in_dim(receiver_wide, MAXLAG + offset_lag, cells_x, 1)]
    dynamic_slice x17 -> x0, other arithmetic: 61.6 us -> none  [step(): lax.dynamic_slice_in_dim(receiver_wide, MAXLAG + offset_lag, cells_x, 1)]
    while x205 -> x0, local copies, waits for them, and re-layouts: 54.7 us -> none
    dynamic_update_slice x34 -> x0, other arithmetic: 46.9 us -> none  [place_add(): return lax.dynamic_update_slice_in_dim(totals, current + values, start, 1)]
    another operation x1 -> x0, loops' own time: 46 us -> none  [local(): source_total, receiver_total = lax.fori_loop(0, NOFF, step, (zeros, zeros))]
    pallas_call x0 -> x6, Pallas kernels: none -> 42.1 us  [image(): pl.pallas_call(image_kernel, out_shape=jax.ShapeDtypeStruct((cells, rows,...]
    ppermute x6 -> x28, waiting for transfers between devices: 181 us -> 143 us  [local(): send = lambda value, route: lax.ppermute(value, ('gx', 'gy'), routes[route])]
    ppermute x6 -> x28, starting transfers between devices: 56.6 us -> 37.9 us  [local(): send = lambda value, route: lax.ppermute(value, ('gx', 'gy'), routes[route])]
  transfers between devices with their start and end apart: 6 -> 28, of which waited for: 6 -> 15; matrix products, arithmetic and copies ran while one was open for 1% -> 4% of each run, Pallas kernels for 0% -> 13%
where the time goes in v1:
time: 264 us
  waiting for transfers between devices  143 us (54%)
  Pallas kernels  42.1 us (16%)
  starting transfers between devices  37.9 us (14%)
  between operations  18.1 us (7%)
  other arithmetic  13.1 us (5%)
  local copies, waits for them, and re-layouts  9.83 us (4%)
    ppermute x28, waiting for transfers between devices, local(): send = lambda value, route: lax.ppermute(value, ('gx', 'gy'), routes[route])  143 us
    pallas_call x6, Pallas kernels, image(): pl.pallas_call(image_kernel, out_shape=jax.ShapeDtypeStruct((cells, rows,...  42.1 us
    ppermute x28, starting transfers between devices, local(): send = lambda value, route: lax.ppermute(value, ('gx', 'gy'), routes[route])  37.9 us
  transfers between devices with their start and end apart: 28, of which 15 were waited for; matrix products, arithmetic and copies ran while one was open for 4% of the time, Pallas kernels for 13%

profile of v1, /device:TPU:7, one launch (start us, length us, event | category | flops | bytes accessed | tf_op | source)
XLA Modules:
  0.0 263.5 jit_solution(1926795272254571768)
XLA Ops:
  0.6 1.5 fusion.3
  11.6 1.8 dynamic-slice_bitcast_fusion.3
  13.4 0.8 bitcast_dynamic-update-slice_fusion.5
  16.1 2.7 %dynamic-slice_bitcast_fusion = (f32[48,16,256]{2,1,0:T(8,128)S(1)}, f32[48,16,256]{2,1,0:T(8,128)}, f32[48,16,256]{2,1,0:T(8,128)S(1)}) fusion(f32[4,48,16,256]{3,2,1,0:T(8,128)} %param.6, s32[]{:T(128)S(6)} %select_n.157, s32[]{:T(128)S(6)} %select_n.149, s32[]{:T(128)S(6)} %select_n.153), kind=kLoop, calls=%fused_computation.2 | loop fusion | bytes 4718604 | tf_op jit(solution)/shard_map/squeeze | solution.py:136
  18.8 1.9 bitcast_dynamic-update-slice_fusion.4
  20.7 0.7 bitcast_dynamic-update-slice_fusion.3
  21.4 0.8 bitcast_dynamic-update-slice_fusion.2
  22.2 0.8 bitcast_dynamic-update-slice_fusion.1
  23.0 0.8 bitcast_dynamic-update-slice_fusion
  23.8 5.4 %collective-permute-start.3 = (f32[6,48,2,256]{3,2,1,0:T(2,128)}, f32[6,48,2,256]{3,2,1,0:T(2,128)}, u32[]{:S(2)}, u32[]{:S(2)}) collective-permute-start(f32[6,48,2,256]{3,2,1,0:T(2,128)} %get-tuple-element.8), channel_id=1, source_target_pairs={{1,2},{2,1},{5,6},{6,5},{9,10},{10,9},{13,14},{14,13},{17,18},{18,... | collective-permute-start | bytes 1769480 | tf_op jit(solution)/shard_map/ppermute | solution.py:128
  29.1 0.5 collective-permute-start.16
  29.6 1.1 collective-permute-start.20
  30.7 0.4 collective-permute-start.24
  31.1 0.7 fusion.4
  37.6 0.1 pad_add_fusion.place
  37.7 5.6 %collective-permute-done.3 = f32[6,48,2,256]{3,2,1,0:T(2,128)} collective-permute-done((f32[6,48,2,256]{3,2,1,0:T(2,128)}, f32[6,48,2,256]{3,2,1,0:T(2,128)}, u32[]{:S(2)}, u32[]{:S(2)}) %collective-permute-start.3) | collective-permute-done | bytes 589856 | tf_op jit(solution)/shard_map/ppermute | solution.py:128
  43.3 1.1 collective-permute-start
  44.5 1.3 slice_bitcast_fusion.18
  45.8 0.4 collective-permute-start.8
  46.2 1.3 slice_bitcast_fusion.19
  47.6 13.1 %collective-permute-done.16.near = f32[48,16,256]{2,1,0:T(8,128)} collective-permute-done((f32[48,16,256]{2,1,0:T(8,128)}, f32[48,16,256]{2,1,0:T(8,128)}, u32[]{:S(2)}, u32[]{:S(2)}) %collective-permute-start.16) | collective-permute-done | bytes 786464 | tf_op jit(solution)/shard_map/ppermute | solution.py:128
  60.6 1.1 collective-permute-start.12
  61.7 1.2 slice_select_fusion.5
  62.9 14.6 %collective-permute-done.20.near = f32[48,16,256]{2,1,0:T(8,128)} collective-permute-done((f32[48,16,256]{2,1,0:T(8,128)S(1)}, f32[48,16,256]{2,1,0:T(8,128)}, u32[]{:S(2)}, u32[]{:S(2)}) %collective-permute-start.20) | collective-permute-done | bytes 786464 | tf_op jit(solution)/shard_map/ppermute | solution.py:128
  77.5 3.0 %collective-permute-start.5 = (f32[6,48,2,256]{3,2,1,0:T(2,128)}, f32[6,48,2,256]{3,2,1,0:T(2,128)S(1)}, u32[]{:S(2)}, u32[]{:S(2)}) collective-permute-start(f32[6,48,2,256]{3,2,1,0:T(2,128)} %collective-permute-done.3), channel_id=1, source_target_pairs={{1,5},{2,6},{5,1},{6,2},{9,13},{10,14},{13,9},{14,10},{17,21},{18,... | collective-permute-start | bytes 1769480 | tf_op jit(solution)/shard_map/ppermute | solution.py:128
  80.5 1.2 slice_select_fusion.3
  81.6 12.6 %collective-permute-done.24.near = f32[48,16,256]{2,1,0:T(8,128)} collective-permute-done((f32[48,16,256]{2,1,0:T(8,128)S(1)}, f32[48,16,256]{2,1,0:T(8,128)}, u32[]{:S(2)}, u32[]{:S(2)}) %collective-permute-start.24) | collective-permute-done | bytes 786464 | tf_op jit(solution)/shard_map/ppermute | solution.py:128
  94.2 1.2 slice_select_fusion.1
  95.4 15.7 %collective-permute-done.near = f32[48,16,256]{2,1,0:T(8,128)S(1)} collective-permute-done((f32[48,16,256]{2,1,0:T(8,128)}, f32[48,16,256]{2,1,0:T(8,128)S(1)}, u32[]{:S(2)}, u32[]{:S(2)}) %collective-permute-start) | collective-permute-done | bytes 786464 | tf_op jit(solution)/shard_map/ppermute | solution.py:128
  111.1 3.5 %collective-permute-start.17 = (f32[48,16,256]{2,1,0:T(8,128)}, f32[48,16,256]{2,1,0:T(8,128)S(1)}, u32[]{:S(2)}, u32[]{:S(2)}) collective-permute-start(f32[48,16,256]{2,1,0:T(8,128)} %collective-permute-done.16.near), channel_id=1, source_target_pairs={{0,8},{1,9},{2,10},{3,11},{8,16},{9,17},{10,18},{11,19},{16,24},{1... | collective-permute-start | bytes 2359304 | tf_op jit(solution)/shard_map/ppermute | solution.py:128
  114.6 0.1 slice_select_fusion.11
  114.7 13.2 %collective-permute-done.8.near = f32[48,16,256]{2,1,0:T(8,128)S(1)} collective-permute-done((f32[48,16,256]{2,1,0:T(8,128)S(1)}, f32[48,16,256]{2,1,0:T(8,128)S(1)}, u32[]{:S(2)}, u32[]{:S(2)}) %collective-permute-start.8) | collective-permute-done | bytes 786464 | tf_op jit(solution)/shard_map/ppermute | solution.py:128
  127.9 3.5 %collective-permute-start.21 = (f32[48,16,256]{2,1,0:T(8,128)}, f32[48,16,256]{2,1,0:T(8,128)S(1)}, u32[]{:S(2)}, u32[]{:S(2)}) collective-permute-start(f32[48,16,256]{2,1,0:T(8,128)} %collective-permute-done.20.near), channel_id=1, source_target_pairs={{0,8},{1,9},{2,10},{3,11},{8,16},{9,17},{10,18},{11,19},{16,24},{1... | collective-permute-start | bytes 2359304 | tf_op jit(solution)/shard_map/ppermute | solution.py:128
  131.5 5.2 %collective-permute-done.12.near = f32[48,16,256]{2,1,0:T(8,128)S(1)} collective-permute-done((f32[48,16,256]{2,1,0:T(8,128)S(1)}, f32[48,16,256]{2,1,0:T(8,128)S(1)}, u32[]{:S(2)}, u32[]{:S(2)}) %collective-permute-start.12) | collective-permute-done | bytes 786464 | tf_op jit(solution)/shard_map/ppermute | solution.py:128
  136.7 3.5 %collective-permute-start.25 = (f32[48,16,256]{2,1,0:T(8,128)}, f32[48,16,256]{2,1,0:T(8,128)S(1)}, u32[]{:S(2)}, u32[]{:S(2)}) collective-permute-start(f32[48,16,256]{2,1,0:T(8,128)} %collective-permute-done.24.near), channel_id=1, source_target_pairs={{0,8},{1,9},{2,10},{3,11},{8,16},{9,17},{10,18},{11,19},{16,24},{1... | collective-permute-start | bytes 2359304 | tf_op jit(solution)/shard_map/ppermute | solution.py:128
  140.3 2.7 %collective-permute-done.5 = f32[6,48,2,256]{3,2,1,0:T(2,128)S(1)} collective-permute-done((f32[6,48,2,256]{3,2,1,0:T(2,128)}, f32[6,48,2,256]{3,2,1,0:T(2,128)S(1)}, u32[]{:S(2)}, u32[]{:S(2)}) %collective-permute-start.5) | collective-permute-done | bytes 589856 | tf_op jit(solution)/shard_map/ppermute | solution.py:128
  143.0 3.5 %collective-permute-start.1 = (f32[48,16,256]{2,1,0:T(8,128)S(1)}, f32[48,16,256]{2,1,0:T(8,128)S(1)}, u32[]{:S(2)}, u32[]{:S(2)}) collective-permute-start(f32[48,16,256]{2,1,0:T(8,128)S(1)} %collective-permute-done.near), channel_id=1, source_target_pairs={{0,8},{1,9},{2,10},{3,11},{8,16},{9,17},{10,18},{11,19},{16,24},{1... | collective-permute-start | bytes 2359304 | tf_op jit(solution)/shard_map/ppermute | solution.py:128
  146.6 0.2 slice_bitcast_fusion.5
  146.8 3.5 %collective-permute-start.9 = (f32[48,16,256]{2,1,0:T(8,128)S(1)}, f32[48,16,256]{2,1,0:T(8,128)S(1)}, u32[]{:S(2)}, u32[]{:S(2)}) collective-permute-start(f32[48,16,256]{2,1,0:T(8,128)S(1)} %collective-permute-done.8.near), channel_id=1, source_target_pairs={{0,8},{1,9},{2,10},{3,11},{8,16},{9,17},{10,18},{11,19},{16,24},{1... | collective-permute-start | bytes 2359304 | tf_op jit(solution)/shard_map/ppermute | solution.py:128
  150.4 0.4 collective-permute-done.21.far
  150.8 2.8 %collective-permute-start.13 = (f32[48,16,256]{2,1,0:T(8,128)S(1)}, f32[48,16,256]{2,1,0:T(8,128)S(1)}, u32[]{:S(2)}, u32[]{:S(2)}) collective-permute-start(f32[48,16,256]{2,1,0:T(8,128)S(1)} %collective-permute-done.12.near), channel_id=1, source_target_pairs={{0,8},{1,9},{2,10},{3,11},{8,16},{9,17},{10,18},{11,19},{16,24},{1... | collective-permute-start | bytes 2359304 | tf_op jit(solution)/shard_map/ppermute | solution.py:128
  153.8 13.9 %collective-permute-done.25.far = f32[48,16,256]{2,1,0:T(8,128)S(1)} collective-permute-done((f32[48,16,256]{2,1,0:T(8,128)}, f32[48,16,256]{2,1,0:T(8,128)S(1)}, u32[]{:S(2)}, u32[]{:S(2)}) %collective-permute-start.25) | collective-permute-done | bytes 786464 | tf_op jit(solution)/shard_map/ppermute | solution.py:128
  167.8 16.8 %collective-permute-done.1.far = f32[48,16,256]{2,1,0:T(8,128)S(1)} collective-permute-done((f32[48,16,256]{2,1,0:T(8,128)S(1)}, f32[48,16,256]{2,1,0:T(8,128)S(1)}, u32[]{:S(2)}, u32[]{:S(2)}) %collective-permute-start.1) | collective-permute-done | bytes 786464 | tf_op jit(solution)/shard_map/ppermute | solution.py:128
  184.5 1.9 collective-permute-start.7
  186.5 14.9 %collective-permute-done.9.far = f32[48,16,256]{2,1,0:T(8,128)S(1)} collective-permute-done((f32[48,16,256]{2,1,0:T(8,128)S(1)}, f32[48,16,256]{2,1,0:T(8,128)S(1)}, u32[]{:S(2)}, u32[]{:S(2)}) %collective-permute-start.9) | collective-permute-done | bytes 786464 | tf_op jit(solution)/shard_map/ppermute | solution.py:128
  201.5 0.6 collective-permute-start.19
  202.1 8.8 %collective-permute-done.13.far = f32[48,16,256]{2,1,0:T(8,128)S(1)} collective-permute-done((f32[48,16,256]{2,1,0:T(8,128)S(1)}, f32[48,16,256]{2,1,0:T(8,128)S(1)}, u32[]{:S(2)}, u32[]{:S(2)}) %collective-permute-start.13) | collective-permute-done | bytes 786464 | tf_op jit(solution)/shard_map/ppermute | solution.py:128
  210.9 0.6 collective-permute-start.26
  211.5 0.1 collective-permute-start.10
  211.6 0.4 collective-permute-start.23
  212.0 0.1 collective-permute-done.6.far_twin
  212.2 0.2 collective-permute-start.27
  212.3 4.9 %collective-permute-done.7 = f32[6,48,2,256]{3,2,1,0:T(2,128)S(1)} collective-permute-done((f32[6,48,2,256]{3,2,1,0:T(2,128)S(1)}, f32[6,48,2,256]{3,2,1,0:T(2,128)S(1)}, u32[]{:S(2)}, u32[]{:S(2)}) %collective-permute-start.7) | collective-permute-done | bytes 589856 | tf_op jit(solution)/shard_map/ppermute | solution.py:128
  217.2 0.2 slice_bitcast_fusion.4
  217.4 7.6 %shard_map.80 = f32[48,16,256]{2,1,0:T(8,128)S(1)} custom-call(s32[2]{0:T(128)S(1)} %pad_add_fusion.place, s32[17]{0:T(128)S(1)} %get-tuple-element.53.lags, f32[17]{0:T(128)S(1)} %get-tuple-element.44.weights, s32[1]{0:T(128)} %constant.35.clone.1.user, f32[48,16,256]{2,1,0:T(8,128)} %get-tuple-element.3.mate.own, ...), custom_call_target="tpu_custom_call" | custom-call | flops 22000000 | bytes 4000000 | tf_op jit(solution)/shard_map/pallas_call | solution.py:106
  225.0 6.7 %shard_map.77 = f32[48,16,256]{2,1,0:T(8,128)S(1)} custom-call(s32[2]{0:T(128)S(1)} %pad_add_fusion.place, s32[17]{0:T(128)S(1)} %get-tuple-element.54.lags, f32[17]{0:T(128)S(1)} %get-tuple-element.44.weights, s32[1]{0:T(128)} %constant.35.clone.1.user, f32[48,16,256]{2,1,0:T(8,128)S(1)} %copy-done.1, f32[48,16,256]{2,1,0:T(8,128)S(1)} %collective-permute-done.near, ...), custom_call_target="tpu_custom_call" | custom-call | flops 22000000 | bytes 4000000 | tf_op jit(solution)/shard_map/pallas_call | solution.py:106
  231.8 0.6 collective-permute-start.14
  232.4 7.1 %shard_map.81 = f32[48,16,256]{2,1,0:T(8,128)S(1)} custom-call(s32[2]{0:T(128)S(1)} %pad_add_fusion.place, s32[17]{0:T(128)S(1)} %get-tuple-element.53.lags, f32[17]{0:T(128)S(1)} %get-tuple-element.46.weights, s32[1]{0:T(128)} %constant.35.clone.1.user, f32[48,16,256]{2,1,0:T(8,128)S(1)} %get-tuple-element.4.mate.own, ...), custom_call_target="tpu_custom_call" | custom-call | flops 22000000 | bytes 4000000 | tf_op jit(solution)/shard_map/pallas_call | solution.py:106
  239.5 0.1 collective-permute-start.15
  239.6 6.8 %shard_map.78 = f32[48,16,256]{2,1,0:T(8,128)S(1)} custom-call(s32[2]{0:T(128)S(1)} %pad_add_fusion.place, s32[17]{0:T(128)S(1)} %get-tuple-element.54.lags, f32[17]{0:T(128)S(1)} %get-tuple-element.46.weights, s32[1]{0:T(128)} %constant.35.clone.1.user, f32[48,16,256]{2,1,0:T(8,128)S(1)} %get-tuple-element.5.own.mate, ...), custom_call_target="tpu_custom_call" | custom-call | flops 22000000 | bytes 4000000 | tf_op jit(solution)/shard_map/pallas_call | solution.py:106
  246.4 7.1 %shard_map.82 = f32[48,16,256]{2,1,0:T(8,128)S(1)} custom-call(s32[2]{0:T(128)S(1)} %pad_add_fusion.place, s32[17]{0:T(128)S(1)} %get-tuple-element.53.lags, f32[17]{0:T(128)S(1)} %get-tuple-element.45.weights, s32[1]{0:T(128)} %constant.35.clone.1.user, f32[48,16,256]{2,1,0:T(8,128)S(1)} %get-tuple-element.2.mate.own, ...), custom_call_target="tpu_custom_call" | custom-call | flops 22000000 | bytes 4000000 | tf_op jit(solution)/shard_map/pallas_call | solution.py:106
  253.5 1.6 pad_maximum_fusion.1
  255.1 6.8 %shard_map.79 = f32[48,16,256]{2,1,0:T(8,128)S(1)} custom-call(s32[2]{0:T(128)S(1)} %pad_add_fusion.place, s32[17]{0:T(128)S(1)} %get-tuple-element.54.lags, f32[17]{0:T(128)S(1)} %get-tuple-element.45.weights, s32[1]{0:T(128)} %constant.35.clone.1.user, f32[48,16,256]{2,1,0:T(8,128)S(1)} %get-tuple-element.7.own.mate, ...), custom_call_target="tpu_custom_call" | custom-call | flops 22000000 | bytes 4000000 | tf_op jit(solution)/shard_map/pallas_call | solution.py:106
  261.9 1.6 pad_maximum_fusion
  (39 shorter events, 0.5 us)
Async XLA Ops:
  13.4 2.1 copy-start
  16.1 15.0 %copy-start.2 = (s32[3]{0:T(128)S(1)}, s32[3]{0:T(128)}, u32[]{:S(2)}) copy-start(s32[3]{0:T(128)} %param.11) | copy-start | bytes 40
  16.1 21.5 %copy-start.3 = (f32[4,17]{1,0:T(4,128)S(1)}, f32[4,17]{1,0:T(4,128)}, u32[]{:S(2)}) copy-start(f32[4,17]{1,0:T(4,128)} %param.10) | copy-start | bytes 820
  16.1 21.5 %copy-start.4 = (s32[17]{0:T(128)S(1)}, s32[17]{0:T(128)}, u32[]{:S(2)}) copy-start(s32[17]{0:T(128)} %param.9) | copy-start | bytes 208
  23.8 19.6 %collective-permute-start.3 = (f32[6,48,2,256]{3,2,1,0:T(2,128)}, f32[6,48,2,256]{3,2,1,0:T(2,128)}, u32[]{:S(2)}, u32[]{:S(2)}) collective-permute-start(f32[6,48,2,256]{3,2,1,0:T(2,128)} %get-tuple-element.8), channel_id=1, source_target_pairs={{1,2},{2,1},{5,6},{6,5},{9,10},{10,9},{13,14},{14,13},{17,18},{18,... | collective-permute-start | bytes 1769480 | tf_op jit(solution)/shard_map/ppermute | solution.py:128
  29.1 31.5 %collective-permute-start.16 = (f32[48,16,256]{2,1,0:T(8,128)}, f32[48,16,256]{2,1,0:T(8,128)}, u32[]{:S(2)}, u32[]{:S(2)}) collective-permute-start(f32[48,16,256]{2,1,0:T(8,128)} %get-tuple-element.3.mate.own), channel_id=1, source_target_pairs={{0,4},{1,5},{2,6},{3,7},{4,0},{5,1},{6,2},{7,3},{8,12},{9,13},{10,... | collective-permute-start | bytes 2359304 | tf_op jit(solution)/shard_map/ppermute | solution.py:128
  29.6 47.9 %collective-permute-start.20 = (f32[48,16,256]{2,1,0:T(8,128)S(1)}, f32[48,16,256]{2,1,0:T(8,128)}, u32[]{:S(2)}, u32[]{:S(2)}) collective-permute-start(f32[48,16,256]{2,1,0:T(8,128)S(1)} %get-tuple-element.4.mate.own), channel_id=1, source_target_pairs={{0,4},{1,5},{2,6},{3,7},{4,0},{5,1},{6,2},{7,3},{8,12},{9,13},{10,... | collective-permute-start | bytes 2359304 | tf_op jit(solution)/shard_map/ppermute | solution.py:128
  30.7 63.5 %collective-permute-start.24 = (f32[48,16,256]{2,1,0:T(8,128)S(1)}, f32[48,16,256]{2,1,0:T(8,128)}, u32[]{:S(2)}, u32[]{:S(2)}) collective-permute-start(f32[48,16,256]{2,1,0:T(8,128)S(1)} %get-tuple-element.2.mate.own), channel_id=1, source_target_pairs={{0,4},{1,5},{2,6},{3,7},{4,0},{5,1},{6,2},{7,3},{8,12},{9,13},{10,... | collective-permute-start | bytes 2359304 | tf_op jit(solution)/shard_map/ppermute | solution.py:128
  31.1 14.7 %collective-permute-start.2 = (f32[6,48,2,256]{3,2,1,0:T(2,128)}, f32[6,48,2,256]{3,2,1,0:T(2,128)}, u32[]{:S(2)}, u32[]{:S(2)}) collective-permute-start(f32[6,48,2,256]{3,2,1,0:T(2,128)} %get-tuple-element.9), channel_id=1, source_target_pairs={{0,1},{1,0},{2,3},{3,2},{4,5},{5,4},{6,7},{7,6},{8,9},{9,8},{10,11... | collective-permute-start | bytes 1769480 | tf_op jit(solution)/shard_map/ppermute | solution.py:128
  43.3 67.8 %collective-permute-start = (f32[48,16,256]{2,1,0:T(8,128)}, f32[48,16,256]{2,1,0:T(8,128)S(1)}, u32[]{:S(2)}, u32[]{:S(2)}) collective-permute-start(f32[48,16,256]{2,1,0:T(8,128)} %copy-done), channel_id=1, source_target_pairs={{0,4},{1,5},{2,6},{3,7},{4,0},{5,1},{6,2},{7,3},{8,12},{9,13},{10,... | collective-permute-start | bytes 2359304 | tf_op jit(solution)/shard_map/ppermute | solution.py:128
  45.8 82.1 %collective-permute-start.8 = (f32[48,16,256]{2,1,0:T(8,128)S(1)}, f32[48,16,256]{2,1,0:T(8,128)S(1)}, u32[]{:S(2)}, u32[]{:S(2)}) collective-permute-start(f32[48,16,256]{2,1,0:T(8,128)S(1)} %get-tuple-element.5.own.mate), channel_id=1, source_target_pairs={{0,4},{1,5},{2,6},{3,7},{4,0},{5,1},{6,2},{7,3},{8,12},{9,13},{10,... | collective-permute-start | bytes 2359304 | tf_op jit(solution)/shard_map/ppermute | solution.py:128
  60.6 76.1 %collective-permute-start.12 = (f32[48,16,256]{2,1,0:T(8,128)S(1)}, f32[48,16,256]{2,1,0:T(8,128)S(1)}, u32[]{:S(2)}, u32[]{:S(2)}) collective-permute-start(f32[48,16,256]{2,1,0:T(8,128)S(1)} %get-tuple-element.7.own.mate), channel_id=1, source_target_pairs={{0,4},{1,5},{2,6},{3,7},{4,0},{5,1},{6,2},{7,3},{8,12},{9,13},{10,... | collective-permute-start | bytes 2359304 | tf_op jit(solution)/shard_map/ppermute | solution.py:128
  77.5 65.6 %collective-permute-start.5 = (f32[6,48,2,256]{3,2,1,0:T(2,128)}, f32[6,48,2,256]{3,2,1,0:T(2,128)S(1)}, u32[]{:S(2)}, u32[]{:S(2)}) collective-permute-start(f32[6,48,2,256]{3,2,1,0:T(2,128)} %collective-permute-done.3), channel_id=1, source_target_pairs={{1,5},{2,6},{5,1},{6,2},{9,13},{10,14},{13,9},{14,10},{17,21},{18,... | collective-permute-start | bytes 1769480 | tf_op jit(solution)/shard_map/ppermute | solution.py:128
  94.2 107.2 %collective-permute-start.18 = (f32[48,2,256]{2,1,0:T(2,128)S(1)}, f32[48,2,256]{2,1,0:T(2,128)S(1)}, u32[]{:S(2)}, u32[]{:S(2)}) collective-permute-start(f32[48,2,256]{2,1,0:T(2,128)S(1)} %slice_select_fusion.5), channel_id=1, source_target_pairs={{0,1},{1,0},{2,3},{3,2},{4,5},{5,4},{6,7},{7,6},{8,9},{9,8},{10,11... | collective-permute-start | bytes 294920 | tf_op jit(solution)/shard_map/ppermute | solution.py:128
  111.1 35.7 %collective-permute-start.17 = (f32[48,16,256]{2,1,0:T(8,128)}, f32[48,16,256]{2,1,0:T(8,128)S(1)}, u32[]{:S(2)}, u32[]{:S(2)}) collective-permute-start(f32[48,16,256]{2,1,0:T(8,128)} %collective-permute-done.16.near), channel_id=1, source_target_pairs={{0,8},{1,9},{2,10},{3,11},{8,16},{9,17},{10,18},{11,19},{16,24},{1... | collective-permute-start | bytes 2359304 | tf_op jit(solution)/shard_map/ppermute | solution.py:128
  114.7 102.7 %copy-start.1 = (f32[48,16,256]{2,1,0:T(8,128)S(1)}, f32[48,16,256]{2,1,0:T(8,128)}, u32[]{:S(2)}) copy-start(f32[48,16,256]{2,1,0:T(8,128)} %copy-done) | copy-start | bytes 2359300
  127.9 22.9 %collective-permute-start.21 = (f32[48,16,256]{2,1,0:T(8,128)}, f32[48,16,256]{2,1,0:T(8,128)S(1)}, u32[]{:S(2)}, u32[]{:S(2)}) collective-permute-start(f32[48,16,256]{2,1,0:T(8,128)} %collective-permute-done.20.near), channel_id=1, source_target_pairs={{0,8},{1,9},{2,10},{3,11},{8,16},{9,17},{10,18},{11,19},{16,24},{1... | collective-permute-start | bytes 2359304 | tf_op jit(solution)/shard_map/ppermute | solution.py:128
  136.7 31.0 %collective-permute-start.25 = (f32[48,16,256]{2,1,0:T(8,128)}, f32[48,16,256]{2,1,0:T(8,128)S(1)}, u32[]{:S(2)}, u32[]{:S(2)}) collective-permute-start(f32[48,16,256]{2,1,0:T(8,128)} %collective-permute-done.24.near), channel_id=1, source_target_pairs={{0,8},{1,9},{2,10},{3,11},{8,16},{9,17},{10,18},{11,19},{16,24},{1... | collective-permute-start | bytes 2359304 | tf_op jit(solution)/shard_map/ppermute | solution.py:128
  143.0 41.5 %collective-permute-start.1 = (f32[48,16,256]{2,1,0:T(8,128)S(1)}, f32[48,16,256]{2,1,0:T(8,128)S(1)}, u32[]{:S(2)}, u32[]{:S(2)}) collective-permute-start(f32[48,16,256]{2,1,0:T(8,128)S(1)} %collective-permute-done.near), channel_id=1, source_target_pairs={{0,8},{1,9},{2,10},{3,11},{8,16},{9,17},{10,18},{11,19},{16,24},{1... | collective-permute-start | bytes 2359304 | tf_op jit(solution)/shard_map/ppermute | solution.py:128
  146.8 54.6 %collective-permute-start.9 = (f32[48,16,256]{2,1,0:T(8,128)S(1)}, f32[48,16,256]{2,1,0:T(8,128)S(1)}, u32[]{:S(2)}, u32[]{:S(2)}) collective-permute-start(f32[48,16,256]{2,1,0:T(8,128)S(1)} %collective-permute-done.8.near), channel_id=1, source_target_pairs={{0,8},{1,9},{2,10},{3,11},{8,16},{9,17},{10,18},{11,19},{16,24},{1... | collective-permute-start | bytes 2359304 | tf_op jit(solution)/shard_map/ppermute | solution.py:128
  150.8 60.0 %collective-permute-start.13 = (f32[48,16,256]{2,1,0:T(8,128)S(1)}, f32[48,16,256]{2,1,0:T(8,128)S(1)}, u32[]{:S(2)}, u32[]{:S(2)}) collective-permute-start(f32[48,16,256]{2,1,0:T(8,128)S(1)} %collective-permute-done.12.near), channel_id=1, source_target_pairs={{0,8},{1,9},{2,10},{3,11},{8,16},{9,17},{10,18},{11,19},{16,24},{1... | collective-permute-start | bytes 2359304 | tf_op jit(solution)/shard_map/ppermute | solution.py:128
  167.7 43.2 %collective-permute-start.22 = (f32[48,2,256]{2,1,0:T(2,128)S(1)}, f32[48,2,256]{2,1,0:T(2,128)S(1)}, u32[]{:S(2)}, u32[]{:S(2)}) collective-permute-start(f32[48,2,256]{2,1,0:T(2,128)S(1)} %slice_select_fusion.3), channel_id=1, source_target_pairs={{0,1},{1,0},{2,3},{3,2},{4,5},{5,4},{6,7},{7,6},{8,9},{9,8},{10,11... | collective-permute-start | bytes 294920 | tf_op jit(solution)/shard_map/ppermute | solution.py:128
  184.5 32.6 %collective-permute-start.7 = (f32[6,48,2,256]{3,2,1,0:T(2,128)S(1)}, f32[6,48,2,256]{3,2,1,0:T(2,128)S(1)}, u32[]{:S(2)}, u32[]{:S(2)}) collective-permute-start(f32[6,48,2,256]{3,2,1,0:T(2,128)S(1)} %collective-permute-done.5), channel_id=1, source_target_pairs={{1,9},{2,10},{9,17},{10,18},{17,25},{18,26},{25,33},{26,34},{33,41... | collective-permute-start | bytes 1769480 | tf_op jit(solution)/shard_map/ppermute | solution.py:128
  201.4 10.1 %collective-permute-start.4 = (f32[48,2,256]{2,1,0:T(2,128)S(1)}, f32[48,2,256]{2,1,0:T(2,128)S(1)}, u32[]{:S(2)}, u32[]{:S(2)}) collective-permute-start(f32[48,2,256]{2,1,0:T(2,128)S(1)} %slice_select_fusion.11), channel_id=1, source_target_pairs={{0,1},{1,0},{2,3},{3,2},{4,5},{5,4},{6,7},{7,6},{8,9},{9,8},{10,11... | collective-permute-start | bytes 294920 | tf_op jit(solution)/shard_map/ppermute | solution.py:128
  201.5 10.1 %collective-permute-start.19 = (f32[48,2,256]{2,1,0:T(2,128)S(1)}, f32[48,2,256]{2,1,0:T(2,128)S(1)}, u32[]{:S(2)}, u32[]{:S(2)}) collective-permute-start(f32[48,2,256]{2,1,0:T(2,128)S(1)} %slice_select_fusion.4), channel_id=1, source_target_pairs={{0,1},{1,0},{2,3},{3,2},{4,5},{5,4},{6,7},{7,6},{8,9},{9,8},{10,11... | collective-permute-start | bytes 294920 | tf_op jit(solution)/shard_map/ppermute | solution.py:128
  210.9 1.3 collective-permute-start.6
  210.9 35.5 %collective-permute-start.26 = (f32[48,2,256]{2,1,0:T(2,128)S(1)}, f32[48,2,256]{2,1,0:T(2,128)S(1)}, u32[]{:S(2)}, u32[]{:S(2)}) collective-permute-start(f32[48,2,256]{2,1,0:T(2,128)S(1)} %slice_select_fusion.1), channel_id=1, source_target_pairs={{0,1},{1,0},{2,3},{3,2},{4,5},{5,4},{6,7},{7,6},{8,9},{9,8},{10,11... | collective-permute-start | bytes 294920 | tf_op jit(solution)/shard_map/ppermute | solution.py:128
  211.5 28.0 %collective-permute-start.10 = (f32[48,2,256]{2,1,0:T(2,128)S(1)}, f32[48,2,256]{2,1,0:T(2,128)S(1)}, u32[]{:S(2)}, u32[]{:S(2)}) collective-permute-start(f32[48,2,256]{2,1,0:T(2,128)S(1)} %slice_select_fusion.9), channel_id=1, source_target_pairs={{0,1},{1,0},{2,3},{3,2},{4,5},{5,4},{6,7},{7,6},{8,9},{9,8},{10,11... | collective-permute-start | bytes 294920 | tf_op jit(solution)/shard_map/ppermute | solution.py:128
  211.6 20.2 %collective-permute-start.23 = (f32[48,2,256]{2,1,0:T(2,128)S(1)}, f32[48,2,256]{2,1,0:T(2,128)S(1)}, u32[]{:S(2)}, u32[]{:S(2)}) collective-permute-start(f32[48,2,256]{2,1,0:T(2,128)S(1)} %slice_select_fusion.2), channel_id=1, source_target_pairs={{0,1},{1,0},{2,3},{3,2},{4,5},{5,4},{6,7},{7,6},{8,9},{9,8},{10,11... | collective-permute-start | bytes 294920 | tf_op jit(solution)/shard_map/ppermute | solution.py:128
  212.2 34.2 %collective-permute-start.27 = (f32[48,2,256]{2,1,0:T(2,128)S(1)}, f32[48,2,256]{2,1,0:T(2,128)S(1)}, u32[]{:S(2)}, u32[]{:S(2)}) collective-permute-start(f32[48,2,256]{2,1,0:T(2,128)S(1)} %slice_select_fusion), channel_id=1, source_target_pairs={{0,1},{1,0},{2,3},{3,2},{4,5},{5,4},{6,7},{7,6},{8,9},{9,8},{10,11... | collective-permute-start | bytes 294920 | tf_op jit(solution)/shard_map/ppermute | solution.py:128
  217.2 22.4 %collective-permute-start.11 = (f32[48,2,256]{2,1,0:T(2,128)S(1)}, f32[48,2,256]{2,1,0:T(2,128)S(1)}, u32[]{:S(2)}, u32[]{:S(2)}) collective-permute-start(f32[48,2,256]{2,1,0:T(2,128)S(1)} %slice_select_fusion.8), channel_id=1, source_target_pairs={{0,1},{1,0},{2,3},{3,2},{4,5},{5,4},{6,7},{7,6},{8,9},{9,8},{10,11... | collective-permute-start | bytes 294920 | tf_op jit(solution)/shard_map/ppermute | solution.py:128
  231.8 23.3 %collective-permute-start.14 = (f32[48,2,256]{2,1,0:T(2,128)S(1)}, f32[48,2,256]{2,1,0:T(2,128)S(1)}, u32[]{:S(2)}, u32[]{:S(2)}) collective-permute-start(f32[48,2,256]{2,1,0:T(2,128)S(1)} %slice_select_fusion.7), channel_id=1, source_target_pairs={{0,1},{1,0},{2,3},{3,2},{4,5},{5,4},{6,7},{7,6},{8,9},{9,8},{10,11... | collective-permute-start | bytes 294920 | tf_op jit(solution)/shard_map/ppermute | solution.py:128
  239.5 15.6 %collective-permute-start.15 = (f32[48,2,256]{2,1,0:T(2,128)S(1)}, f32[48,2,256]{2,1,0:T(2,128)S(1)}, u32[]{:S(2)}, u32[]{:S(2)}) collective-permute-start(f32[48,2,256]{2,1,0:T(2,128)S(1)} %slice_select_fusion.6), channel_id=1, source_target_pairs={{0,1},{1,0},{2,3},{3,2},{4,5},{5,4},{6,7},{7,6},{8,9},{9,8},{10,11... | collective-permute-start | bytes 294920 | tf_op jit(solution)/shard_map/ppermute | solution.py:128
